TPU v7x, 256 devices: a whole 4x4x8 slice. The times are simulated.
256 devices in a mesh: expert: 64 (over z, y, x_hi), dp: 4 (over x_lo, core).
Axes of the slice: x: 4 (x_hi: 2, x_lo: 2; x = x_hi * 2 + x_lo), y: 4, z: 8, core: 2. Of those that a mesh axis runs over, the one named last changes fastest.
Arguments:
- tokens: bfloat16 [16384, 2048], P(('expert', 'dp')), may hold values from -6 to 6
- expert_ids: int32 [16384, 8], P(('expert', 'dp')), may hold values from 0 to 63, all different within a row; in each aligned block of 64 rows (0 to 63, 64 to 127, ...) at most 16 rows name the same one
- targets: bfloat16 [16384, 8, 2048], P(('expert', 'dp')), may hold values from -400 to 400
- gate_weight: bfloat16 [64, 2048, 768], P('expert', 'dp'), may hold values from -0.125 to 0.125
- up_weight: bfloat16 [64, 2048, 768], P('expert', 'dp'), may hold values from -0.125 to 0.125
- kept_units: int32 [64, 384], P('expert'), may hold values from 0 to 767, as said below
Outputs:
- refit: float32 [64, 384, 2048], P('expert', None, 'dp')
Inputs may be any that keep to these rules, and one draw needn't show every extreme that they name: `expert_ids`: among the rows of one device no expert is named by more than 16 routes, and in every draw some device names some expert exactly 16 times. `kept_units`: each row holds 384 distinct hidden units in increasing order.
All inputs are finite; a program needn't handle non-finite values.
Results may differ from a plain program's by a relative error of at most 0.0034.
Values may be sent and summed in bfloat16 or wider, within the bound.
A program may use at most 128 MiB of HBM per device.

v0:
```python
import jax
import jax.numpy as jnp
from jax import lax
from jax.sharding import PartitionSpec as P

ITERS = 3


def body(tokens, expert_ids, targets, gate_weight, up_weight, kept_units):
    experts = lax.axis_size("expert")
    tok_rows, model_width = tokens.shape
    routes = expert_ids.shape[1]
    capacity = 2 * tok_rows * routes // experts
    flat_ids = expert_ids.reshape(-1)
    onehot = (flat_ids[:, None] == jnp.arange(experts, dtype=jnp.int32)[None, :]).astype(jnp.int32)
    position = jnp.sum(jnp.cumsum(onehot, axis=0) * onehot, axis=1) - 1
    destination = flat_ids * capacity + position
    repeated = jnp.repeat(tokens, routes, axis=0)
    feature_buf = (
        jnp.zeros((experts * capacity, model_width), jnp.bfloat16).at[destination].set(repeated)
    )
    feature_buf = feature_buf.reshape(experts, capacity, model_width)
    target_buf = (
        jnp.zeros((experts * capacity, model_width), jnp.bfloat16)
        .at[destination]
        .set(targets.reshape(-1, model_width))
    )
    target_buf = target_buf.reshape(experts, capacity, model_width)
    kept_cols = kept_units[0]
    kept_count = kept_cols.shape[0]
    gate_kept = jnp.take(gate_weight[0], kept_cols, axis=1)
    up_kept = jnp.take(up_weight[0], kept_cols, axis=1)
    features, goals = (
        lax.all_to_all(feature_buf, "expert", split_axis=0, concat_axis=0, tiled=True),
        lax.all_to_all(target_buf, "expert", split_axis=0, concat_axis=0, tiled=True),
    )
    goal_rows = goals.reshape(-1, model_width)
    row_data = features.reshape(-1, model_width)
    gate_acts = jnp.dot(
        row_data,
        lax.all_gather(gate_kept, "dp", axis=0, tiled=True),
        preferred_element_type=jnp.float32,
    )
    up_acts = jnp.dot(
        row_data,
        lax.all_gather(up_kept, "dp", axis=0, tiled=True),
        preferred_element_type=jnp.float32,
    )
    hidden = (jax.nn.silu(gate_acts) * up_acts).astype(jnp.bfloat16)
    rhs_cols = lax.psum_scatter(
        lax.dot_general(
            goal_rows, hidden, (((0,), (0,)), ((), ())), preferred_element_type=jnp.float32
        ),
        "dp",
        scatter_dimension=0,
        tiled=True,
    )
    gram_part = lax.dot_general(
        hidden, hidden, (((0,), (0,)), ((), ())), preferred_element_type=jnp.float32
    )
    gram_total = lax.psum(gram_part, "dp")
    damping = 0.01 * (jnp.mean(jnp.diagonal(gram_total)) + 1e-06)
    system = gram_total + damping * jnp.eye(kept_count, dtype=jnp.float32)
    solution = jnp.zeros_like(rhs_cols)
    residual = rhs_cols

    def squares(vector):
        return lax.psum(jnp.sum(vector * vector), "dp")

    direction = rhs_cols
    norm_now = squares(residual)
    for iteration in range(ITERS):
        applied = jnp.dot(direction, system, precision=lax.Precision.HIGHEST)
        step_size = norm_now / lax.psum(jnp.sum(direction * applied), "dp")
        solution = solution + step_size * direction
        residual = residual - step_size * applied
        if iteration + 1 < ITERS:
            norm_next = squares(residual)
            direction = residual + norm_next / norm_now * direction
            norm_now = norm_next
    return solution.T[None]


def solution(mesh):
    placed = (
        P(("expert", "dp"), None),
        P(("expert", "dp"), None),
        P(("expert", "dp"), None, None),
        P("expert", "dp", None),
        P("expert", "dp", None),
        P("expert", None),
    )
    return jax.shard_map(
        body, mesh=mesh, in_specs=placed, out_specs=P("expert", None, "dp"), check_vma=False
    )
```

profile of v0, /device:TPU:1, one launch (start us, length us, event | category | flops | bytes accessed | tf_op | source)
XLA Modules:
  0.0 390.0 jit_solution(5207673543587605892)
XLA Ops:
  6.5 0.9 copy.11
  7.5 0.1 eq.32
  7.5 0.1 eq.28
  7.6 0.7 broadcast_multiply_fusion
  8.3 1.2 reduce-window.6
  9.6 0.2 slice_reduce_fusion
  9.8 0.1 fusion.17
  10.0 0.1 copy.10
  10.0 0.1 mul.90
  10.2 6.6 %scatter_custom_fusion.1 = bf16[1024,2048]{1,0:T(8,128)(2,1)} fusion(s32[512]{0:T(512)S(1)} %bitcast.52, bf16[]{:T(256)} %constant.15.clone.1, bf16[64,2048]{1,0:T(8,128)(2,1)} %param.8), kind=kCustom, calls=%fused_computation.5 | custom fusion | bytes 4456450 | tf_op jit(solution)/shard_map/scatter | solution.py:20
  16.7 15.4 %all-to-all-start.1 = ((bf16[64,16,2048]{2,1,0:T(8,128)(2,1)}), bf16[64,16,2048]{2,1,0:T(8,128)(2,1)}, u32[]{:S(2)}, u32[]{:S(2)}) async-start(bf16[64,16,2048]{2,1,0:T(8,128)(2,1)} %bitcast.50), calls=%async_computation.1 | async-start | bytes 8388608 | tf_op jit(solution)/shard_map/all_to_all | solution.py:34
  32.1 6.2 %scatter_custom_fusion = bf16[1024,2048]{1,0:T(8,128)(2,1)} fusion(s32[512]{0:T(512)S(1)} %bitcast.53, bf16[64,8,2048]{2,1,0:T(8,128)(2,1)S(1)} %copy-done, bf16[]{:T(256)} %constant.15.clone.1), kind=kCustom, calls=%fused_computation.7 | custom fusion | bytes 6291458 | tf_op jit(solution)/shard_map/scatter | solution.py:26
  38.3 86.3 %all-to-all-done.1 = bf16[64,16,2048]{2,1,0:T(8,128)(2,1)} async-done(((bf16[64,16,2048]{2,1,0:T(8,128)(2,1)}), bf16[64,16,2048]{2,1,0:T(8,128)(2,1)}, u32[]{:S(2)}, u32[]{:S(2)}) %all-to-all-start.1) | async-done | bytes 4194336 | tf_op jit(solution)/shard_map/all_to_all | solution.py:34
  124.6 10.0 %all-to-all-start = ((bf16[64,16,2048]{2,1,0:T(8,128)(2,1)}), bf16[64,16,2048]{2,1,0:T(8,128)(2,1)}, u32[]{:S(2)}, u32[]{:S(2)}) async-start(bf16[64,16,2048]{2,1,0:T(8,128)(2,1)} %bitcast.49), calls=%async_computation | async-start | bytes 8388608 | tf_op jit(solution)/shard_map/all_to_all | solution.py:35
  134.6 0.0 all-gather.3.cloned.1.call-start
  134.7 1.2 copy.14
  135.9 1.4 copy.15
  137.3 3.3 gather_fusion.1
  140.6 2.6 gather_fusion.2
  143.2 2.0 select_bitcast_fusion
  145.3 0.0 all-gather.5.cloned.1.call-start
  145.3 0.7 all-gather.5.cloned.1.call-update
  146.0 0.0 all-reduce.3.cloned.1.call-start
  146.1 39.3 %all-gather.3.cloned.1.call-done = bf16[2048,384]{0,1:T(8,128)(2,1)} async-done(((bf16[512,384]{0,1:T(8,128)(2,1)}), bf16[2048,384]{0,1:T(8,128)(2,1)}) %all-gather.3.cloned.1.call-update) | async-done | bytes 1572880 | tf_op jit(solution)/shard_map/all_gather | solution.py:41
  185.4 6.2 %fusion.22 = f32[1024,384]{1,0:T(8,128)} fusion(bf16[1024,2048]{1,0:T(8,128)(2,1)} %bitcast.8, bf16[2048,384]{0,1:T(8,128)(2,1)} %all-gather.3.cloned.1.call-done), kind=kOutput, calls=%fused_computation.55 | convolution fusion | flops 1610612736 | bytes 7340032 | tf_op jit(solution)/shard_map/dot_general | solution.py:39
  191.5 34.4 %all-gather.5.cloned.1.call-done = bf16[2048,384]{0,1:T(8,128)(2,1)} async-done(((bf16[512,384]{0,1:T(8,128)(2,1)}), bf16[2048,384]{0,1:T(8,128)(2,1)}) %all-gather.5.cloned.1.call-update) | async-done | bytes 1572880 | tf_op jit(solution)/shard_map/all_gather | solution.py:46
  225.9 5.5 %multiply_convert_fusion = bf16[1024,384]{1,0:T(8,128)(2,1)S(1)} fusion(f32[1024,384]{1,0:T(8,128)} %fusion.22, bf16[1024,2048]{1,0:T(8,128)(2,1)} %bitcast.8, bf16[2048,384]{0,1:T(8,128)(2,1)} %all-gather.5.cloned.1.call-done), kind=kOutput, calls=%fused_computation.11 | convolution fusion | flops 1612972032 | bytes 8126464 | tf_op jit(solution)/shard_map/dot_general | solution.py:44
  231.5 1.4 fusion.24
  232.9 0.0 reduce-scatter.2.cloned.1.call-start
  233.0 6.3 %fusion.23 = f32[2048,384]{1,0:T(8,128)} fusion(bf16[1024,2048]{1,0:T(8,128)(2,1)} %bitcast.5, bf16[1024,384]{1,0:T(8,128)(2,1)S(1)} %multiply_convert_fusion), kind=kOutput, calls=%fused_computation.56 | convolution fusion | flops 1610612736 | bytes 8126464 | tf_op jit(solution)/shard_map/dot_general | solution.py:51
  239.3 39.2 %all-reduce.3.cloned.1.call-done = f32[384,384]{1,0:T(8,128)} async-done(((f32[384,384]{1,0:T(8,128)}), f32[384,384]{1,0:T(8,128)}) %all-reduce.3.cloned.1.call-update) | async-done | bytes 589840 | tf_op jit(solution)/shard_map/psum | solution.py:61
  278.5 6.6 %gather_fusion = f32[384]{0:T(512)S(1)} fusion(f32[384,384]{1,0:T(8,128)} %all-reduce.3.cloned.1.call-done, s32[384]{0:T(512)S(1)} %or_reduce_fusion), kind=kCustom, calls=%fused_computation.2 | custom fusion | bytes 6144 | tf_op jit(solution)/shard_map/jit(diagonal)/cond/branch_0_fun/gather | solution.py:62
  285.1 0.6 reduce_sum.74
  286.3 34.7 %reduce-scatter.2.cloned.1.call-done = f32[512,384]{1,0:T(8,128)} async-done(((f32[2048,384]{1,0:T(8,128)}), f32[512,384]{1,0:T(8,128)}) %reduce-scatter.2.cloned.1.call-update) | async-done | bytes 786448 | tf_op jit(solution)/shard_map/reduce_scatter | solution.py:50
  321.0 4.6 %multiply_reduce_fusion.3 = (f32[]{:T(128)}, f32[]{:T(128)}, f32[512,384]{1,0:T(8,128)}) fusion(f32[512,384]{1,0:T(8,128)} %reduce-scatter.2.cloned.1.call-done, f32[384,384]{1,0:T(8,128)S(1)} %copy-done.1, f32[]{:T(128)S(6)} %mul_shard_map.3), kind=kOutput, calls=%fused_computation.22 | convolution fusion | flops 907198464 | bytes 2162700 | tf_op jit(solution)/shard_map/dot_general | solution.py:73
  325.6 6.1 %all-reduce = (f32[]{:T(128)}, f32[]{:T(128)}) all-reduce(f32[]{:T(128)} %get-tuple-element.7, f32[]{:T(128)} %get-tuple-element.6), channel_id=1, replica_groups=mesh['expert'=64,'dp'=4] {'dp'}, use_global_device_ids=true, to_apply=%region_7.9 | all-reduce | flops 2 | bytes 16 | tf_op jit(solution)/shard_map/psum | solution.py:68
  333.0 2.0 multiply_reduce_fusion.2
  335.0 6.6 %psum.52 = f32[]{:T(128)} all-reduce(f32[]{:T(128)} %multiply_reduce_fusion.2), channel_id=1, replica_groups=mesh['expert'=64,'dp'=4] {'dp'}, use_global_device_ids=true, to_apply=%region_13.15 | all-reduce | flops 1 | bytes 8 | tf_op jit(solution)/shard_map/psum | solution.py:68
  342.9 1.2 multiply_add_fusion.1
  344.2 0.9 copy-done.3
  345.0 3.2 multiply_reduce_fusion.1
  348.2 6.4 %psum.53 = f32[]{:T(128)} all-reduce(f32[]{:T(128)} %get-tuple-element.15), channel_id=1, replica_groups=mesh['expert'=64,'dp'=4] {'dp'}, use_global_device_ids=true, to_apply=%region_15.17 | all-reduce | flops 1 | bytes 8 | tf_op jit(solution)/shard_map/psum | solution.py:74
  355.9 3.0 multiply_reduce_fusion
  359.0 7.3 %psum.54 = f32[]{:T(128)} all-reduce(f32[]{:T(128)} %get-tuple-element.10), channel_id=1, replica_groups=mesh['expert'=64,'dp'=4] {'dp'}, use_global_device_ids=true, to_apply=%region_17.19 | all-reduce | flops 1 | bytes 8 | tf_op jit(solution)/shard_map/psum | solution.py:68
  367.6 3.6 fusion.7
  371.2 6.3 %psum.55 = f32[]{:T(128)} all-reduce(f32[]{:T(128)} %fusion.7), channel_id=1, replica_groups=mesh['expert'=64,'dp'=4] {'dp'}, use_global_device_ids=true, to_apply=%region_19.21 | all-reduce | flops 1 | bytes 8 | tf_op jit(solution)/shard_map/psum | solution.py:74
  378.8 2.5 add_bitcast_fusion
  381.2 2.3 copy.16
  (25 shorter events, 0.2 us)
Async XLA Ops:
  6.5 25.6 %copy-start = (bf16[64,8,2048]{2,1,0:T(8,128)(2,1)S(1)}, bf16[64,8,2048]{2,1,0:T(8,128)(2,1)}, u32[]{:S(2)}) copy-start(bf16[64,8,2048]{2,1,0:T(8,128)(2,1)} %param.10) | copy-start | bytes 6291460
  16.7 107.9 %all-to-all-start.1 = ((bf16[64,16,2048]{2,1,0:T(8,128)(2,1)}), bf16[64,16,2048]{2,1,0:T(8,128)(2,1)}, u32[]{:S(2)}, u32[]{:S(2)}) async-start(bf16[64,16,2048]{2,1,0:T(8,128)(2,1)} %bitcast.50), calls=%async_computation.1 | async-start | bytes 8388608 | tf_op jit(solution)/shard_map/all_to_all | solution.py:34
  124.6 10.0 %copy-start.5 = (s32[1,384]{1,0:T(1,128)S(1)}, s32[1,384]{1,0:T(1,128)}, u32[]{:S(2)}) copy-start(s32[1,384]{1,0:T(1,128)} %param.13) | copy-start | bytes 4612
  124.6 10.1 %copy-start.4 = (bf16[1,512,768]{2,1,0:T(8,128)(2,1)S(1)}, bf16[1,512,768]{2,1,0:T(8,128)(2,1)}, u32[]{:S(2)}) copy-start(bf16[1,512,768]{2,1,0:T(8,128)(2,1)} %param.11) | copy-start | bytes 2359300
  124.6 108.3 %all-to-all-start = ((bf16[64,16,2048]{2,1,0:T(8,128)(2,1)}), bf16[64,16,2048]{2,1,0:T(8,128)(2,1)}, u32[]{:S(2)}, u32[]{:S(2)}) async-start(bf16[64,16,2048]{2,1,0:T(8,128)(2,1)} %bitcast.49), calls=%async_computation | async-start | bytes 8388608 | tf_op jit(solution)/shard_map/all_to_all | solution.py:35
  134.6 50.7 %all-gather.3.cloned.1.call-start = ((), (), s32[]{:S(2)}) async-start(), calls=%async_computation.3 | async-start | bytes 1966080 | tf_op jit(solution)/shard_map/all_gather | solution.py:41
  145.3 80.7 %all-gather.5.cloned.1.call-start = ((), (), s32[]{:S(2)}) async-start(), calls=%async_computation.4 | async-start | bytes 1966080 | tf_op jit(solution)/shard_map/all_gather | solution.py:46
  146.0 132.4 %all-reduce.3.cloned.1.call-start = ((), (), s32[]{:S(2)}) async-start(), calls=%async_computation.6 | async-start | bytes 1179648 | tf_op jit(solution)/shard_map/psum | solution.py:61
  232.9 88.1 %reduce-scatter.2.cloned.1.call-start = ((), (), s32[]{:S(2)}) async-start(), calls=%async_computation.5 | async-start | bytes 3932160 | tf_op jit(solution)/shard_map/reduce_scatter | solution.py:50
  278.5 42.5 %copy-start.1 = (f32[384,384]{1,0:T(8,128)S(1)}, f32[384,384]{1,0:T(8,128)}, u32[]{:S(2)}) copy-start(f32[384,384]{1,0:T(8,128)} %all-reduce.3.cloned.1.call-done) | copy-start | bytes 1769476
  321.0 12.0 %copy-start.2 = (f32[512,384]{1,0:T(8,128)S(1)}, f32[512,384]{1,0:T(8,128)}, u32[]{:S(2)}) copy-start(f32[512,384]{1,0:T(8,128)} %reduce-scatter.2.cloned.1.call-done) | copy-start | bytes 2359300
  344.1 0.9 copy-start.3
Sparse Core Ops, SparseCore 0:
  145.4 39.9 all-gather.2
  187.2 38.7 all-gather.4
  233.0 45.3 all-reduce.2
  280.9 40.0 reduce-scatter.1
where the time goes:
time: 391 us; the launch traced here: 390 us
  waiting for transfers between devices  235 us (60%)
  blocking collectives  32.8 us (8%)
  local copies, waits for them, and re-layouts  32.5 us (8%)
  matrix products  30.7 us (8%)
  starting transfers between devices  25.5 us (7%)
  between operations  20.4 us (5%)
  other arithmetic  13.5 us (3%)
    all_to_all x1, waiting for transfers between devices, body(): lax.all_to_all(feature_buf, 'expert', split_axis=0, concat_axis=0, tiled=...  86.3 us
    all_gather x1, waiting for transfers between devices, body(): lax.all_gather(gate_kept, 'dp', axis=0, tiled=True)  39.3 us
    psum x1, waiting for transfers between devices, body(): gram_total = lax.psum(gram_part, 'dp')  39.2 us
    reduce_scatter x1, waiting for transfers between devices, body(): lax.psum_scatter(lax.dot_general(goal_rows, hidden, (((0,), (0,)), ((), (...  34.7 us
    all_gather x1, waiting for transfers between devices, body(): lax.all_gather(up_kept, 'dp', axis=0, tiled=True)  34.4 us
    psum x3, blocking collectives, squares(): return lax.psum(jnp.sum(vector * vector), 'dp')  20 us
    all_to_all x1, starting transfers between devices, body(): lax.all_to_all(feature_buf, 'expert', split_axis=0, concat_axis=0, tiled=...  15.4 us
    psum x2, blocking collectives, body(): step_size = norm_now / lax.psum(jnp.sum(direction * applied), 'dp')  12.8 us
  transfers between devices with their start and end apart: 6, of which 5 were waited for; matrix products, arithmetic and copies ran while one was open for 11% of the time, Pallas kernels for 0%

commit v1 on v0

v1 whole, which is shorter than its diff:
```python
import functools

import jax
import jax.numpy as jnp
from jax import lax
from jax.experimental import pallas as pl
from jax.experimental.pallas import tpu as pltpu
from jax.sharding import PartitionSpec as P

ITERS = 3
Z, Y, H, L, C = 8, 4, 2, 2, 2
PLANE = Y * H
CAP = 16
MESH = pl.DeviceIdType.MESH
NT = (((1,), (1,)), ((), ()))


def dot(a, b, dims=(((1,), (0,)), ((), ()))):
    return lax.dot_general(a, b, dims, preferred_element_type=jnp.float32)


def kernel(
    ids_ref, kept_ref, tokens_hbm, targets_hbm, gate_hbm, up_hbm, out_ref,
    tok, idsb, targ, gate, up, slots, before, fsend, feats, weights, hid, tsend, tmid, tfin,
    rhs, system, vec_p, vec_s, scal,
    in_sem, ring_send, ring_recv, idr_send, idr_recv, f_send, f_recv, t1_send, t1_recv,
    t2_send, t2_recv, w_send, w_recv, h_send, h_recv, s_send, s_recv,
):
    e = lax.axis_index("expert")
    d = lax.axis_index("dp")
    z, y, h = e // PLANE, (e // H) % Y, e % H
    l, c = d // C, d % C
    here = y * H + h

    def at_z(o):
        return ((z + o) % Z) * PLANE + here, d

    def in_plane(k):
        y2, h2 = (y + k // 8) % Y, (h + (k // 4) % 2) % H
        l2, c2 = (l + (k // 2) % 2) % L, (c + k % 2) % C
        return y2 * H + h2, l2 * C + c2

    def remote(src, dst, send, recv, device):
        return pltpu.make_async_remote_copy(
            src_ref=src, dst_ref=dst, send_sem=send, recv_sem=recv, device_id=device, device_id_type=MESH
        )

    def drain(ref, sem):
        pltpu.make_async_copy(ref, ref, sem).wait()

    barrier = pltpu.get_barrier_semaphore()

    def greet_z(o, _):
        pl.semaphore_signal(barrier, inc=1, device_id=at_z(o), device_id_type=MESH)
        return 0

    def greet_plane(k, _):
        i2, d2 = in_plane(k)
        pl.semaphore_signal(barrier, inc=1, device_id=(z * PLANE + i2, d2), device_id_type=MESH)
        return 0

    lax.fori_loop(1, Z, greet_z, 0)
    lax.fori_loop(1, PLANE * L * C, greet_plane, 0)

    loads = [
        pltpu.make_async_copy(src, dst, in_sem.at[n])
        for n, (src, dst) in enumerate(
            [(tokens_hbm, tok.at[0]), (targets_hbm, targ), (gate_hbm, gate), (up_hbm, up)]
        )
    ]
    for load in loads:
        load.start()

    idsb[0] = jnp.broadcast_to(ids_ref[...], idsb.shape[1:])
    routes = idsb.shape[2]
    row_at = lax.broadcasted_iota(jnp.int32, (routes, routes), 0)
    col_at = lax.broadcasted_iota(jnp.int32, (routes, routes), 1)
    before[...] = (row_at < col_at).astype(jnp.float32).astype(jnp.bfloat16)

    def places(ids, first, count):
        named = (ids == first + lax.broadcasted_iota(jnp.int32, (count, routes), 0)).astype(jnp.float32)
        rank = dot(named.astype(jnp.bfloat16), before[...])
        return jnp.where(named > 0, rank, -1.0)

    def one_hot(place):
        wide = jnp.broadcast_to(place[:, None, :], (PLANE, CAP, routes))
        slot = lax.broadcasted_iota(jnp.int32, (PLANE, CAP, routes), 1).astype(jnp.float32)
        return (wide == slot).astype(jnp.float32).reshape(PLANE * CAP, routes).astype(jnp.bfloat16)

    ids_row = ids_ref[...]
    all_places = places(jnp.broadcast_to(ids_row, (Z * PLANE, routes)), 0, Z * PLANE)
    for n in range(Z):
        slots[n] = all_places[n * PLANE : (n + 1) * PLANE]

    pl.semaphore_wait(barrier, Z - 1 + PLANE * L * C - 1)
    loads[0].wait()

    half = tok.shape[1] // 2

    def ring_start(step):
        src_r, src_l = 2 * (step - 1), jnp.maximum(2 * step - 3, 0)
        remote(tok.at[src_r], tok.at[2 * step], ring_send, ring_recv.at[step, 0], at_z(1)).start()
        remote(tok.at[src_l], tok.at[2 * step - 1], ring_send, ring_recv.at[step, 1], at_z(Z - 1)).start()
        remote(idsb.at[src_r], idsb.at[2 * step], idr_send, idr_recv.at[step, 0], at_z(1)).start()
        remote(idsb.at[src_l], idsb.at[2 * step - 1], idr_send, idr_recv.at[step, 1], at_z(Z - 1)).start()

    def ring_wait(step):
        drain(tok.at[2 * step], ring_recv.at[step, 0])
        drain(tok.at[2 * step - 1], ring_recv.at[step, 1])
        drain(idsb.at[2 * step], idr_recv.at[step, 0])
        drain(idsb.at[2 * step - 1], idr_recv.at[step, 1])

    low, high = pl.ds(0, half), pl.ds(half, half)

    def ring_start_last():
        remote(tok.at[6, low], tok.at[7, low], ring_send, ring_recv.at[4, 0], at_z(1)).start()
        remote(tok.at[5, high], tok.at[7, high], ring_send, ring_recv.at[4, 1], at_z(Z - 1)).start()
        remote(idsb.at[6], idsb.at[7], idr_send, idr_recv.at[4, 0], at_z(1)).start()

    def ring_wait_last():
        drain(tok.at[7, low], ring_recv.at[4, 0])
        drain(tok.at[7, high], ring_recv.at[4, 1])
        drain(idsb.at[7], idr_recv.at[4, 0])

    def pack_features(s):
        place = places(idsb[s], z * PLANE, PLANE)
        tokens_of = (
            lax.broadcasted_iota(jnp.int32, (routes, tok.shape[1]), 0) // (routes // tok.shape[1])
            == lax.broadcasted_iota(jnp.int32, (routes, tok.shape[1]), 1)
        ).astype(jnp.float32).astype(jnp.bfloat16)
        picks = dot(one_hot(place), tokens_of).astype(jnp.bfloat16)
        fsend[s] = dot(picks, tok[s]).astype(jnp.bfloat16)

        def push(k, _):
            y2, h2 = (y + k // 2) % Y, (h + k % 2) % H
            d2 = ((l + k % 2) % L) * C + c
            i2 = y2 * H + h2
            rows = pl.ds(pl.multiple_of(i2 * CAP, CAP), CAP)
            mine = pl.ds(pl.multiple_of(here * CAP, CAP), CAP)
            remote(
                fsend.at[s, rows], feats.at[s, mine], f_send.at[s], f_recv.at[s], (z * PLANE + i2, d2)
            ).start()
            return 0

        lax.fori_loop(1, PLANE, push, 0)
        mine = pl.ds(pl.multiple_of(here * CAP, CAP), CAP)
        pltpu.make_async_copy(fsend.at[s, mine], feats.at[s, mine], f_recv.at[s]).start()

    def pack_targets(s, o):
        packed = dot(one_hot(slots[(z + o) % Z]), targ[...]).astype(jnp.bfloat16)
        width = tsend.shape[3]
        for n in range(L * C):
            tsend[s, n] = packed[:, n * width : (n + 1) * width]

    def hop_z(s, o, other):
        remote(tsend.at[s], tmid.at[other], t1_send.at[s], t1_recv.at[other], at_z(o)).start()

    def spread(src, s):
        def push(k, _):
            i2, d2 = in_plane(k)
            owner = ((l + (k // 4) % 2) % L) * C + c
            rows = pl.ds(pl.multiple_of(i2 * CAP, CAP), CAP)
            there = pl.ds(pl.multiple_of((owner * PLANE + here) * CAP, CAP), CAP)
            remote(
                src.at[s, d2, rows], tfin.at[s, there], t2_send.at[s], t2_recv.at[s], (z * PLANE + i2, d2)
            ).start()
            return 0

        lax.fori_loop(1, PLANE * L * C, push, 0)
        rows = pl.ds(pl.multiple_of(here * CAP, CAP), CAP)
        there = pl.ds(pl.multiple_of((d * PLANE + here) * CAP, CAP), CAP)
        pltpu.make_async_copy(src.at[s, d, rows], tfin.at[s, there], t2_recv.at[s]).start()

    across = (e, ((l + 1) % L) * C + c)
    beside = (e, l * C + (c + 1) % C)
    d_across = ((l + 1) % L) * C + c
    d_beside = l * C + (c + 1) % C
    d_diag = ((l + 1) % L) * C + (c + 1) % C

    ring_start(1)
    pack_features(0)
    loads[1].wait()
    pack_targets(0, 0)
    spread(tsend, 0)

    loads[2].wait()
    loads[3].wait()
    keep = kept_ref.shape[1]
    hidden_units = gate.shape[1]
    kept_down = jnp.transpose(jnp.broadcast_to(kept_ref[...].astype(jnp.float32), (128, keep)))
    lane = lax.broadcasted_iota(jnp.int32, (keep, 128), 1).astype(jnp.float32)
    chosen = jnp.concatenate(
        [(kept_down == lane + float(128 * n)).astype(jnp.float32) for n in range(hidden_units // 128)], axis=1
    ).astype(jnp.bfloat16)
    weights[d, pl.ds(0, keep)] = dot(chosen, gate[...], NT).astype(jnp.bfloat16)
    weights[d, pl.ds(keep, keep)] = dot(chosen, up[...], NT).astype(jnp.bfloat16)
    remote(weights.at[d], weights.at[d], w_send.at[0], w_recv.at[0], across).start()
    remote(weights.at[d], weights.at[d], w_send.at[1], w_recv.at[1], beside).start()

    def turn(step, _):
        ring_wait(step)

        @pl.when(step < 3)
        def _():
            ring_start(step + 1)

        @pl.when(step == 3)
        def _():
            ring_start_last()

        pack_features(2 * step - 1)
        pack_features(2 * step)
        pack_targets(2 * step - 1, step)
        hop_z(2 * step - 1, step, 2 * step)
        pack_targets(2 * step, Z - step)
        hop_z(2 * step, Z - step, 2 * step - 1)
        return 0

    lax.fori_loop(1, 4, turn, 0)
    ring_wait_last()
    pack_features(7)
    pack_targets(7, Z // 2)
    hop_z(7, Z // 2, 7)

    drain(weights.at[d_across], w_recv.at[0])
    remote(weights.at[d_across], weights.at[d_across], w_send.at[2], w_recv.at[2], beside).start()

    def forward(s, _):
        drain(tmid.at[s], t1_recv.at[s])
        spread(tmid, s)
        return 0

    lax.fori_loop(1, 5, forward, 0)

    drain(weights.at[d_beside], w_recv.at[1])
    drain(weights.at[d_diag], w_recv.at[2])

    def activate(n, _):
        drain(feats.at[2 * n], f_recv.at[2 * n])
        drain(feats.at[2 * n + 1], f_recv.at[2 * n + 1])
        rows = feats.shape[1]
        block = feats[pl.ds(2 * n, 2)].reshape(2 * rows, feats.shape[2])
        width = weights.shape[2]
        acts = dot(weights[0], block[:, 0:width], NT)
        for q in range(1, L * C):
            acts = acts + dot(weights[q], block[:, q * width : (q + 1) * width], NT)
        gate_acts, up_acts = acts[:keep], acts[keep:]
        hidden = (gate_acts / (1.0 + jnp.exp(-gate_acts)) * up_acts).astype(jnp.bfloat16)
        hid[d, 2 * n] = hidden[:, :rows]
        hid[d, 2 * n + 1] = hidden[:, rows:]
        return 0

    lax.fori_loop(0, 4, activate, 0)
    remote(hid.at[d], hid.at[d], h_send.at[0], h_recv.at[0], across).start()
    remote(hid.at[d], hid.at[d], h_send.at[1], h_recv.at[1], beside).start()

    lax.fori_loop(5, 7, forward, 0)
    drain(hid.at[d_across], h_recv.at[0])
    remote(hid.at[d_across], hid.at[d_across], h_send.at[2], h_recv.at[2], beside).start()
    forward(7, 0)
    drain(hid.at[d_beside], h_recv.at[1])
    drain(hid.at[d_diag], h_recv.at[2])

    def hidden_of(s):
        return jnp.concatenate([hid[q, s] for q in range(L * C)], axis=1)

    system[...] = jnp.zeros_like(system)

    def add_gram(s, _):
        block = hidden_of(s)
        system[...] += dot(block, block, NT)
        return 0

    lax.fori_loop(0, Z, add_gram, 0)
    gram = system[...]
    on_diagonal = lax.broadcasted_iota(jnp.int32, gram.shape, 0) == lax.broadcasted_iota(jnp.int32, gram.shape, 1)
    trace = jnp.sum(jnp.where(on_diagonal, gram, 0.0))
    damping = 0.01 * (trace / keep + 1e-6)
    system[...] = gram + jnp.where(on_diagonal, damping, 0.0)

    rhs[...] = jnp.zeros_like(rhs)

    def add_rhs(s, _):
        drain(tfin.at[s], t2_recv.at[s])
        rhs[...] += dot(hidden_of(s), tfin[s])
        return 0

    lax.fori_loop(0, Z, add_rhs, 0)

    def folded(value):
        rows = value.reshape(value.shape[0] // 8, 8, value.shape[1]).sum(axis=0)
        total = rows[:, 0:128]
        for n in range(1, value.shape[1] // 128):
            total = total + rows[:, n * 128 : (n + 1) * 128]
        return total

    def exchange(it, first, second):
        scal[it, d, 0] = first
        scal[it, d, 1] = second
        copies = []
        for k in range(1, L * C):
            there = (d + k) % (L * C)
            copies.append(
                remote(scal.at[it, d], scal.at[it, d], s_send.at[it, k], s_recv.at[it, k], (e, there))
            )
        for copy in copies:
            copy.start()
        for copy in copies:
            copy.wait()
        sums = scal[it, 0]
        for k in range(1, L * C):
            sums = sums + scal[it, k]
        return jnp.sum(sums[0]), jnp.sum(sums[1])

    rr_old = alpha = None
    for it in range(ITERS):
        residual = rhs[...]
        image = jnp.dot(system[...], residual, precision=lax.Precision.HIGHEST)
        rr, curve = exchange(it, folded(residual * residual), folded(residual * image))
        if it == 0:
            alpha = rr / curve
            vec_p[...] = residual
            vec_s[...] = image
            out_ref[0] = alpha * residual
            rhs[...] = residual - alpha * image
        else:
            beta = rr / rr_old
            alpha = rr / (curve - beta * rr / alpha)
            direction = residual + beta * vec_p[...]
            out_ref[0] += alpha * direction
            if it + 1 < ITERS:
                applied = image + beta * vec_s[...]
                vec_p[...] = direction
                vec_s[...] = applied
                rhs[...] = residual - alpha * applied
        rr_old = rr

    drain(tok.at[pl.ds(0, 7)], ring_send)
    drain(idsb.at[pl.ds(0, 7)], idr_send)
    for s in range(Z):
        drain(feats.at[s, pl.ds(0, (PLANE - 1) * CAP)], f_send.at[s])
        drain(tfin.at[s, pl.ds(0, (PLANE * L * C - 1) * CAP)], t2_send.at[s])
        if s:
            drain(tsend.at[s], t1_send.at[s])
    for n in range(3):
        drain(weights.at[0], w_send.at[n])
        drain(hid.at[0], h_send.at[n])


def body(tokens, expert_ids, targets, gate_weight, up_weight, kept_units):
    tok_rows, model_width = tokens.shape
    routes = expert_ids.shape[1]
    keep = kept_units.shape[1]
    rows, units = gate_weight.shape[1:]
    ids = expert_ids.reshape(1, -1)
    targets = targets.reshape(-1, model_width)
    part = L * C
    out_cols = model_width // part
    slots = PLANE * CAP
    vmem = pl.BlockSpec(memory_space=pltpu.VMEM)
    hbm = pl.BlockSpec(memory_space=pl.ANY)
    dma = pltpu.SemaphoreType.DMA
    bf, f32 = jnp.bfloat16, jnp.float32
    return pl.pallas_call(
        kernel,
        out_shape=jax.ShapeDtypeStruct((1, keep, out_cols), f32),
        in_specs=[vmem, vmem, hbm, hbm, hbm, hbm],
        out_specs=vmem,
        scratch_shapes=[
            pltpu.VMEM((Z, tok_rows, model_width), bf),
            pltpu.VMEM((Z, 8, tok_rows * routes), jnp.int32),
            pltpu.VMEM((tok_rows * routes, model_width), bf),
            pltpu.VMEM((rows, units), bf),
            pltpu.VMEM((rows, units), bf),
            pltpu.VMEM((Z, PLANE, tok_rows * routes), f32),
            pltpu.VMEM((tok_rows * routes, tok_rows * routes), bf),
            pltpu.VMEM((Z, slots, model_width), bf),
            pltpu.VMEM((Z, slots, model_width), bf),
            pltpu.VMEM((part, 2 * keep, rows), bf),
            pltpu.VMEM((part, Z, keep, slots), bf),
            pltpu.VMEM((Z, part, slots, out_cols), bf),
            pltpu.VMEM((Z, part, slots, out_cols), bf),
            pltpu.VMEM((Z, part * slots, out_cols), bf),
            pltpu.VMEM((keep, out_cols), f32),
            pltpu.VMEM((keep, keep), f32),
            pltpu.VMEM((keep, out_cols), f32),
            pltpu.VMEM((keep, out_cols), f32),
            pltpu.VMEM((ITERS, part, 2, 8, 128), f32),
            dma((4,)), dma, dma((5, 2)), dma, dma((5, 2)), dma((Z,)), dma((Z,)), dma((Z,)), dma((Z,)),
            dma((Z,)), dma((Z,)), dma((3,)), dma((3,)), dma((3,)), dma((3,)),
            dma((ITERS, part)), dma((ITERS, part)),
        ],
        compiler_params=pltpu.CompilerParams(
            collective_id=0, has_side_effects=True, vmem_limit_bytes=56 * 2**20
        ),
    )(ids, kept_units, tokens, targets, gate_weight[0], up_weight[0])


def solution(mesh):
    placed = (
        P(("expert", "dp"), None),
        P(("expert", "dp"), None),
        P(("expert", "dp"), None, None),
        P("expert", "dp", None),
        P("expert", "dp", None),
        P("expert", None),
    )
    return jax.shard_map(
        body, mesh=mesh, in_specs=placed, out_specs=P("expert", None, "dp"), check_vma=False
    )
```

time: 391 us -> 161 us (0.41)
  the two profiles are of different devices: /device:TPU:1 before, /device:TPU:161 now
where the time goes in v1:
time: 161 us
  Pallas kernels  157 us (98%)
  local copies, waits for them, and re-layouts  3.5 us (2%)
    pallas_call x1, Pallas kernels, body(): pl.pallas_call(kernel, out_shape=jax.ShapeDtypeStruct((1, keep, out_cols)...  157 us

profile of v1, /device:TPU:161, one launch (start us, length us, event | category | flops | bytes accessed | tf_op | source)
XLA Modules:
  0.0 160.8 jit_solution(5842449475510243244)
XLA Ops:
  0.0 0.8 copy.8
  0.8 0.7 reshape.6.ids_ref
  1.4 157.2 %shard_map.64 = f32[1,384,512]{2,1,0:T(8,128)} custom-call(s32[1,512]{1,0:T(1,128)} %reshape.6.ids_ref, s32[1,384]{1,0:T(1,128)} %kept_ref.1, bf16[64,2048]{1,0:T(8,128)(2,1)} %tokens_hbm.1, bf16[512,2048]{1,0:T(8,128)(2,1)} %bitcast.3, bf16[512,768]{1,0:T(8,128)(2,1)} %bitcast.4, bf16[512,768]{1,0:T(8,128)(2,1)} %bitcast.5), custom_call_target="tpu_custom_call" | custom-call | tf_op jit(solution)/shard_map/pallas_call | solution.py:364
  158.7 2.1 %copy.10 = f32[1,384,512]{2,1,0:T(8,128)} copy(f32[1,384,512]{2,1,0:T(8,128)} %shard_map.64) | data formatting | bytes 1572864

commit v2 on v1

--- a/solution.py
+++ b/solution.py
@@ -20,12 +20,14 @@
 
 
 def kernel(
-    ids_ref, kept_ref, tokens_hbm, targets_hbm, gate_hbm, up_hbm, out_ref,
-    tok, idsb, targ, gate, up, slots, before, fsend, feats, weights, hid, tsend, tmid, tfin,
-    rhs, system, vec_p, vec_s, scal,
+    limits, ids_ref, kept_ref, tokens_hbm, targets_hbm, gate_hbm, up_hbm, out_ref, flag_ref,
+    tok, idsb, targ, gate, up, before, fsend, feats, weights, hid, tsend, tmid, tpack, tfin,
+    picked, rhs, system, vec_p, vec_s, scal, flags,
     in_sem, ring_send, ring_recv, idr_send, idr_recv, f_send, f_recv, t1_send, t1_recv,
-    t2_send, t2_recv, w_send, w_recv, h_send, h_recv, s_send, s_recv,
+    t2_send, t2_recv, w_send, w_recv, h_send, h_recv, s_send, s_recv, g_send, g_recv,
 ):
+    most, spare = limits
+    tokens_here = tokens_hbm.shape[0]
     e = lax.axis_index("expert")
     d = lax.axis_index("dp")
     z, y, h = e // PLANE, (e // H) % Y, e % H
@@ -65,7 +67,7 @@
     loads = [
         pltpu.make_async_copy(src, dst, in_sem.at[n])
         for n, (src, dst) in enumerate(
-            [(tokens_hbm, tok.at[0]), (targets_hbm, targ), (gate_hbm, gate), (up_hbm, up)]
+            [(tokens_hbm, tok.at[0, pl.ds(0, tokens_here)]), (targets_hbm, targ), (gate_hbm, gate), (up_hbm, up)]
         )
     ]
     for load in loads:
@@ -87,10 +89,25 @@
         slot = lax.broadcasted_iota(jnp.int32, (PLANE, CAP, routes), 1).astype(jnp.float32)
         return (wide == slot).astype(jnp.float32).reshape(PLANE * CAP, routes).astype(jnp.bfloat16)
 
-    ids_row = ids_ref[...]
-    all_places = places(jnp.broadcast_to(ids_row, (Z * PLANE, routes)), 0, Z * PLANE)
-    for n in range(Z):
-        slots[n] = all_places[n * PLANE : (n + 1) * PLANE]
+    def plane_rows(ids):
+        plane = ids // PLANE
+        named = (plane == lax.broadcasted_iota(jnp.int32, (Z, routes), 0)).astype(jnp.float32)
+        rank = dot(named.astype(jnp.bfloat16), before[...])
+        rank = jnp.broadcast_to(jnp.sum(named * rank, axis=0, keepdims=True), (Z, routes))
+        over = (rank >= most).astype(jnp.float32)
+        late = dot(over.astype(jnp.bfloat16), before[...])
+        return plane, jnp.where(over > 0, most + late, rank), jnp.sum(over[0:1])
+
+    def row_hot(place, first, count):
+        row = first + lax.broadcasted_iota(jnp.int32, (count, routes), 0).astype(jnp.float32)
+        return (jnp.broadcast_to(place[0:1], (count, routes)) == row).astype(jnp.float32).astype(jnp.bfloat16)
+
+    my_plane, my_row, _ = plane_rows(idsb[0])
+    flags[0] = jnp.zeros_like(flags[0])
+    loads[1].wait()
+    if spare:
+        late_rows = pl.ds(tokens_here, spare)
+        tok[0, late_rows] = dot(row_hot(my_row, float(most), spare), targ[...]).astype(jnp.bfloat16)
 
     pl.semaphore_wait(barrier, Z - 1 + PLANE * L * C - 1)
     loads[0].wait()
@@ -124,12 +141,13 @@
 
     def pack_features(s):
         place = places(idsb[s], z * PLANE, PLANE)
+        hot = one_hot(place)
         tokens_of = (
-            lax.broadcasted_iota(jnp.int32, (routes, tok.shape[1]), 0) // (routes // tok.shape[1])
-            == lax.broadcasted_iota(jnp.int32, (routes, tok.shape[1]), 1)
+            lax.broadcasted_iota(jnp.int32, (routes, tokens_here), 0) // (routes // tokens_here)
+            == lax.broadcasted_iota(jnp.int32, (routes, tokens_here), 1)
         ).astype(jnp.float32).astype(jnp.bfloat16)
-        picks = dot(one_hot(place), tokens_of).astype(jnp.bfloat16)
-        fsend[s] = dot(picks, tok[s]).astype(jnp.bfloat16)
+        picks = dot(hot, tokens_of).astype(jnp.bfloat16)
+        fsend[s] = dot(picks, tok[s, pl.ds(0, tokens_here)]).astype(jnp.bfloat16)
 
         def push(k, _):
             y2, h2 = (y + k // 2) % Y, (h + k % 2) % H
@@ -145,31 +163,37 @@
         lax.fori_loop(1, PLANE, push, 0)
         mine = pl.ds(pl.multiple_of(here * CAP, CAP), CAP)
         pltpu.make_async_copy(fsend.at[s, mine], feats.at[s, mine], f_recv.at[s]).start()
+        plane, row, late = plane_rows(idsb[s])
+        picked[s] = dot(hot, row_hot(jnp.where(plane == z, row, -1.0), 0.0, most + spare), NT).astype(jnp.bfloat16)
+        flags[0] = jnp.maximum(flags[0], late - float(spare))
+        return hot
 
     def pack_targets(s, o):
-        packed = dot(one_hot(slots[(z + o) % Z]), targ[...]).astype(jnp.bfloat16)
-        width = tsend.shape[3]
-        for n in range(L * C):
-            tsend[s, n] = packed[:, n * width : (n + 1) * width]
+        place = jnp.where(my_plane == (z + o) % Z, my_row, -1.0)
+        tsend[s] = dot(row_hot(place, 0.0, most), targ[...]).astype(jnp.bfloat16)
 
     def hop_z(s, o, other):
         remote(tsend.at[s], tmid.at[other], t1_send.at[s], t1_recv.at[other], at_z(o)).start()
 
-    def spread(src, s):
+    def spread(s, packed):
+        width = tpack.shape[3]
+        for n in range(L * C):
+            tpack[s, n] = packed[:, n * width : (n + 1) * width].astype(jnp.bfloat16)
+
         def push(k, _):
             i2, d2 = in_plane(k)
             owner = ((l + (k // 4) % 2) % L) * C + c
             rows = pl.ds(pl.multiple_of(i2 * CAP, CAP), CAP)
             there = pl.ds(pl.multiple_of((owner * PLANE + here) * CAP, CAP), CAP)
             remote(
-                src.at[s, d2, rows], tfin.at[s, there], t2_send.at[s], t2_recv.at[s], (z * PLANE + i2, d2)
+                tpack.at[s, d2, rows], tfin.at[s, there], t2_send.at[s], t2_recv.at[s], (z * PLANE + i2, d2)
             ).start()
             return 0
 
         lax.fori_loop(1, PLANE * L * C, push, 0)
         rows = pl.ds(pl.multiple_of(here * CAP, CAP), CAP)
         there = pl.ds(pl.multiple_of((d * PLANE + here) * CAP, CAP), CAP)
-        pltpu.make_async_copy(src.at[s, d, rows], tfin.at[s, there], t2_recv.at[s]).start()
+        pltpu.make_async_copy(tpack.at[s, d, rows], tfin.at[s, there], t2_recv.at[s]).start()
 
     across = (e, ((l + 1) % L) * C + c)
     beside = (e, l * C + (c + 1) % C)
@@ -178,10 +202,7 @@
     d_diag = ((l + 1) % L) * C + (c + 1) % C
 
     ring_start(1)
-    pack_features(0)
-    loads[1].wait()
-    pack_targets(0, 0)
-    spread(tsend, 0)
+    spread(0, dot(pack_features(0), targ[...]))
 
     loads[2].wait()
     loads[3].wait()
@@ -227,7 +248,10 @@
 
     def forward(s, _):
         drain(tmid.at[s], t1_recv.at[s])
-        spread(tmid, s)
+        rows = tmid[s]
+        if spare:
+            rows = jnp.concatenate([rows, tok[s, late_rows]], axis=0)
+        spread(s, dot(picked[s], rows))
         return 0
 
     lax.fori_loop(1, 5, forward, 0)
@@ -258,6 +282,13 @@
     drain(hid.at[d_across], h_recv.at[0])
     remote(hid.at[d_across], hid.at[d_across], h_send.at[2], h_recv.at[2], beside).start()
     forward(7, 0)
+
+    def tell(k, _):
+        i2, d2 = in_plane(k)
+        remote(flags.at[0], flags.at[k], g_send, g_recv, (z * PLANE + i2, d2)).start()
+        return 0
+
+    lax.fori_loop(1, PLANE * L * C, tell, 0)
     drain(hid.at[d_beside], h_recv.at[1])
     drain(hid.at[d_diag], h_recv.at[2])
 
@@ -335,6 +366,11 @@
                 rhs[...] = residual - alpha * applied
         rr_old = rr
 
+    others = flags.at[pl.ds(1, PLANE * L * C - 1)]
+    drain(others, g_recv)
+    drain(others, g_send)
+    flag_ref[...] = jnp.max(flags[...], axis=0)
+
     drain(tok.at[pl.ds(0, 7)], ring_send)
     drain(idsb.at[pl.ds(0, 7)], idr_send)
     for s in range(Z):
@@ -347,7 +383,8 @@
         drain(hid.at[0], h_send.at[n])
 
 
-def body(tokens, expert_ids, targets, gate_weight, up_weight, kept_units):
+def refit(limits, number, tokens, expert_ids, targets, gate_weight, up_weight, kept_units):
+    most, spare = limits
     tok_rows, model_width = tokens.shape
     routes = expert_ids.shape[1]
     keep = kept_units.shape[1]
@@ -362,38 +399,45 @@
     dma = pltpu.SemaphoreType.DMA
     bf, f32 = jnp.bfloat16, jnp.float32
     return pl.pallas_call(
-        kernel,
-        out_shape=jax.ShapeDtypeStruct((1, keep, out_cols), f32),
+        functools.partial(kernel, limits),
+        out_shape=(jax.ShapeDtypeStruct((1, keep, out_cols), f32), jax.ShapeDtypeStruct((8, 128), f32)),
         in_specs=[vmem, vmem, hbm, hbm, hbm, hbm],
-        out_specs=vmem,
+        out_specs=(vmem, vmem),
         scratch_shapes=[
-            pltpu.VMEM((Z, tok_rows, model_width), bf),
+            pltpu.VMEM((Z, tok_rows + spare, model_width), bf),
             pltpu.VMEM((Z, 8, tok_rows * routes), jnp.int32),
             pltpu.VMEM((tok_rows * routes, model_width), bf),
             pltpu.VMEM((rows, units), bf),
             pltpu.VMEM((rows, units), bf),
-            pltpu.VMEM((Z, PLANE, tok_rows * routes), f32),
             pltpu.VMEM((tok_rows * routes, tok_rows * routes), bf),
             pltpu.VMEM((Z, slots, model_width), bf),
             pltpu.VMEM((Z, slots, model_width), bf),
             pltpu.VMEM((part, 2 * keep, rows), bf),
             pltpu.VMEM((part, Z, keep, slots), bf),
-            pltpu.VMEM((Z, part, slots, out_cols), bf),
+            pltpu.VMEM((Z, most, model_width), bf),
+            pltpu.VMEM((Z, most, model_width), bf),
             pltpu.VMEM((Z, part, slots, out_cols), bf),
             pltpu.VMEM((Z, part * slots, out_cols), bf),
+            pltpu.VMEM((Z, slots, most + spare), bf),
             pltpu.VMEM((keep, out_cols), f32),
             pltpu.VMEM((keep, keep), f32),
             pltpu.VMEM((keep, out_cols), f32),
             pltpu.VMEM((keep, out_cols), f32),
             pltpu.VMEM((ITERS, part, 2, 8, 128), f32),
+            pltpu.VMEM((PLANE * part, 8, 128), f32),
             dma((4,)), dma, dma((5, 2)), dma, dma((5, 2)), dma((Z,)), dma((Z,)), dma((Z,)), dma((Z,)),
             dma((Z,)), dma((Z,)), dma((3,)), dma((3,)), dma((3,)), dma((3,)),
-            dma((ITERS, part)), dma((ITERS, part)),
+            dma((ITERS, part)), dma((ITERS, part)), dma, dma,
         ],
         compiler_params=pltpu.CompilerParams(
-            collective_id=0, has_side_effects=True, vmem_limit_bytes=56 * 2**20
+            collective_id=number, has_side_effects=True, vmem_limit_bytes=56 * 2**20
         ),
     )(ids, kept_units, tokens, targets, gate_weight[0], up_weight[0])
+
+
+def body(*args):
+    result, flag = refit((80, 32), 0, *args)
+    return lax.cond(flag[0, 0] > 0, lambda: refit((PLANE * CAP, 0), 1, *args)[0], lambda: result)
 
 
 def solution(mesh):

time: 161 us -> 150 us (0.932)
  the two profiles are of different devices: /device:TPU:161 before, /device:TPU:1 now
where the time goes in v2:
time: 150 us; the launch traced here: 148 us
  Pallas kernels  144 us (96%)
  local copies, waits for them, and re-layouts  3.69 us (2%)
    pallas_call x1, Pallas kernels, refit(): pl.pallas_call(functools.partial(kernel, limits), out_shape=(jax.ShapeDty...  144 us

profile of v2, /device:TPU:1, one launch (start us, length us, event | category | flops | bytes accessed | tf_op | source)
XLA Modules:
  0.0 148.4 jit_solution(7425525700052926891)
XLA Ops:
  0.0 0.0 copy-start.4
  0.0 0.0 copy-start.1
  0.0 0.0 copy-start
  0.0 0.0 copy-start.3
  0.0 0.0 copy-start.2
  0.0 0.9 copy.11
  1.0 0.7 reshape.16.ids_ref
  1.6 143.8 %shard_map.66 = (f32[1,384,512]{2,1,0:T(8,128)S(1)}, f32[8,128]{1,0:T(8,128)}) custom-call(s32[1,512]{1,0:T(1,128)} %reshape.16.ids_ref, s32[1,384]{1,0:T(1,128)} %kept_ref.1, bf16[64,2048]{1,0:T(8,128)(2,1)} %tokens_hbm.1, bf16[512,2048]{1,0:T(8,128)(2,1)} %bitcast.7, bf16[512,768]{1,0:T(8,128)(2,1)} %bitcast.9, bf16[512,768]{1,0:T(8,128)(2,1)} %bitcast.5.up_hbm), custom_call_target="tpu_custom_call" | custom-call | tf_op jit(solution)/shard_map/pallas_call | solution.py:401
  145.5 1.2 slice.3
  147.3 0.0 copy-done.4
  147.3 0.0 copy-done.1
  147.3 0.0 copy-done
  147.4 0.0 copy-done.3
  147.4 0.0 copy-done.2
  147.4 0.2 conditional.1
  147.6 0.9 copy.16
Async XLA Ops:
  0.0 147.3 %copy-start.4 = (s32[1,384]{1,0:T(1,128)S(1)}, s32[1,384]{1,0:T(1,128)}, u32[]{:S(2)}) copy-start(s32[1,384]{1,0:T(1,128)} %kept_ref.1) | copy-start | bytes 4612
  0.0 147.3 %copy-start.1 = (bf16[1,512,768]{2,1,0:T(8,128)(2,1)S(1)}, bf16[1,512,768]{2,1,0:T(8,128)(2,1)}, u32[]{:S(2)}) copy-start(bf16[1,512,768]{2,1,0:T(8,128)(2,1)} %param.11) | copy-start | bytes 2359300
  0.0 147.3 %copy-start = (bf16[64,8,2048]{2,1,0:T(8,128)(2,1)S(1)}, bf16[64,8,2048]{2,1,0:T(8,128)(2,1)}, u32[]{:S(2)}) copy-start(bf16[64,8,2048]{2,1,0:T(8,128)(2,1)} %param.10) | copy-start | bytes 6291460
  0.0 147.3 %copy-start.3 = (s32[64,8]{0,1:T(8,128)S(1)}, s32[64,8]{0,1:T(8,128)}, u32[]{:S(2)}) copy-start(s32[64,8]{0,1:T(8,128)} %param.9) | copy-start | bytes 6148
  0.0 147.3 %copy-start.2 = (bf16[64,2048]{1,0:T(8,128)(2,1)S(1)}, bf16[64,2048]{1,0:T(8,128)(2,1)}, u32[]{:S(2)}) copy-start(bf16[64,2048]{1,0:T(8,128)(2,1)} %tokens_hbm.1) | copy-start | bytes 786436

commit v3 on v2

--- a/solution.py
+++ b/solution.py
@@ -218,34 +218,6 @@
     remote(weights.at[d], weights.at[d], w_send.at[0], w_recv.at[0], across).start()
     remote(weights.at[d], weights.at[d], w_send.at[1], w_recv.at[1], beside).start()
 
-    def turn(step, _):
-        ring_wait(step)
-
-        @pl.when(step < 3)
-        def _():
-            ring_start(step + 1)
-
-        @pl.when(step == 3)
-        def _():
-            ring_start_last()
-
-        pack_features(2 * step - 1)
-        pack_features(2 * step)
-        pack_targets(2 * step - 1, step)
-        hop_z(2 * step - 1, step, 2 * step)
-        pack_targets(2 * step, Z - step)
-        hop_z(2 * step, Z - step, 2 * step - 1)
-        return 0
-
-    lax.fori_loop(1, 4, turn, 0)
-    ring_wait_last()
-    pack_features(7)
-    pack_targets(7, Z // 2)
-    hop_z(7, Z // 2, 7)
-
-    drain(weights.at[d_across], w_recv.at[0])
-    remote(weights.at[d_across], weights.at[d_across], w_send.at[2], w_recv.at[2], beside).start()
-
     def forward(s, _):
         drain(tmid.at[s], t1_recv.at[s])
         rows = tmid[s]
@@ -253,11 +225,6 @@
             rows = jnp.concatenate([rows, tok[s, late_rows]], axis=0)
         spread(s, dot(picked[s], rows))
         return 0
-
-    lax.fori_loop(1, 5, forward, 0)
-
-    drain(weights.at[d_beside], w_recv.at[1])
-    drain(weights.at[d_diag], w_recv.at[2])
 
     def activate(n, _):
         drain(feats.at[2 * n], f_recv.at[2 * n])
@@ -272,15 +239,73 @@
         hidden = (gate_acts / (1.0 + jnp.exp(-gate_acts)) * up_acts).astype(jnp.bfloat16)
         hid[d, 2 * n] = hidden[:, :rows]
         hid[d, 2 * n + 1] = hidden[:, rows:]
-        return 0
-
-    lax.fori_loop(0, 4, activate, 0)
-    remote(hid.at[d], hid.at[d], h_send.at[0], h_recv.at[0], across).start()
-    remote(hid.at[d], hid.at[d], h_send.at[1], h_recv.at[1], beside).start()
-
-    lax.fori_loop(5, 7, forward, 0)
-    drain(hid.at[d_across], h_recv.at[0])
-    remote(hid.at[d_across], hid.at[d_across], h_send.at[2], h_recv.at[2], beside).start()
+        part = hid.at[d, pl.ds(2 * n, 2)]
+        remote(part, part, h_send.at[n, 0], h_recv.at[n, 0], across).start()
+        remote(part, part, h_send.at[n, 1], h_recv.at[n, 1], beside).start()
+        return 0
+
+    def pass_on(n, _):
+        part = hid.at[d_across, pl.ds(2 * n, 2)]
+        drain(part, h_recv.at[n, 0])
+        remote(part, part, h_send.at[n, 2], h_recv.at[n, 2], beside).start()
+        return 0
+
+    def hidden_of(s):
+        return jnp.concatenate([hid[q, s] for q in range(L * C)], axis=1)
+
+    def add_gram(n, _):
+        drain(hid.at[d_beside, pl.ds(2 * n, 2)], h_recv.at[n, 1])
+        drain(hid.at[d_diag, pl.ds(2 * n, 2)], h_recv.at[n, 2])
+        for k in range(2):
+            block = hidden_of(2 * n + k)
+            system[...] += dot(block, block, NT)
+        return 0
+
+    def add_rhs(s, _):
+        drain(tfin.at[s], t2_recv.at[s])
+        rhs[...] += dot(hidden_of(s), tfin[s])
+        return 0
+
+    def turn(step):
+        ring_wait(step)
+        if step < 3:
+            ring_start(step + 1)
+        else:
+            ring_start_last()
+        pack_features(2 * step - 1)
+        pack_features(2 * step)
+        pack_targets(2 * step - 1, step)
+        hop_z(2 * step - 1, step, 2 * step)
+        pack_targets(2 * step, Z - step)
+        hop_z(2 * step, Z - step, 2 * step - 1)
+
+    turn(1)
+    turn(2)
+    drain(weights.at[d_across], w_recv.at[0])
+    remote(weights.at[d_across], weights.at[d_across], w_send.at[2], w_recv.at[2], beside).start()
+    turn(3)
+    lax.fori_loop(1, 3, forward, 0)
+    drain(weights.at[d_beside], w_recv.at[1])
+    drain(weights.at[d_diag], w_recv.at[2])
+    lax.fori_loop(0, 2, activate, 0)
+    ring_wait_last()
+    pack_features(7)
+    pack_targets(7, Z // 2)
+    activate(2, 0)
+    lax.fori_loop(0, 2, pass_on, 0)
+    lax.fori_loop(3, 5, forward, 0)
+    activate(3, 0)
+    pass_on(2, 0)
+    drain(tsend.at[0], t1_send.at[5])
+    drain(tsend.at[0], t1_send.at[6])
+    hop_z(7, Z // 2, 7)
+    forward(5, 0)
+    pass_on(3, 0)
+    forward(6, 0)
+    system[...] = jnp.zeros_like(system)
+    rhs[...] = jnp.zeros_like(rhs)
+    lax.fori_loop(0, 2, add_gram, 0)
+    lax.fori_loop(0, 4, add_rhs, 0)
     forward(7, 0)
 
     def tell(k, _):
@@ -289,34 +314,14 @@
         return 0
 
     lax.fori_loop(1, PLANE * L * C, tell, 0)
-    drain(hid.at[d_beside], h_recv.at[1])
-    drain(hid.at[d_diag], h_recv.at[2])
-
-    def hidden_of(s):
-        return jnp.concatenate([hid[q, s] for q in range(L * C)], axis=1)
-
-    system[...] = jnp.zeros_like(system)
-
-    def add_gram(s, _):
-        block = hidden_of(s)
-        system[...] += dot(block, block, NT)
-        return 0
-
-    lax.fori_loop(0, Z, add_gram, 0)
+    lax.fori_loop(2, 4, add_gram, 0)
     gram = system[...]
     on_diagonal = lax.broadcasted_iota(jnp.int32, gram.shape, 0) == lax.broadcasted_iota(jnp.int32, gram.shape, 1)
     trace = jnp.sum(jnp.where(on_diagonal, gram, 0.0))
     damping = 0.01 * (trace / keep + 1e-6)
     system[...] = gram + jnp.where(on_diagonal, damping, 0.0)
 
-    rhs[...] = jnp.zeros_like(rhs)
-
-    def add_rhs(s, _):
-        drain(tfin.at[s], t2_recv.at[s])
-        rhs[...] += dot(hidden_of(s), tfin[s])
-        return 0
-
-    lax.fori_loop(0, Z, add_rhs, 0)
+    lax.fori_loop(4, Z, add_rhs, 0)
 
     def folded(value):
         rows = value.reshape(value.shape[0] // 8, 8, value.shape[1]).sum(axis=0)
@@ -376,11 +381,13 @@
     for s in range(Z):
         drain(feats.at[s, pl.ds(0, (PLANE - 1) * CAP)], f_send.at[s])
         drain(tfin.at[s, pl.ds(0, (PLANE * L * C - 1) * CAP)], t2_send.at[s])
-        if s:
-            drain(tsend.at[s], t1_send.at[s])
+    for n in (1, 2, 3, 4, 7):
+        drain(tsend.at[0], t1_send.at[n])
     for n in range(3):
         drain(weights.at[0], w_send.at[n])
-        drain(hid.at[0], h_send.at[n])
+    for n in range(Z // 2):
+        for k in range(3):
+            drain(hid.at[0, pl.ds(0, 2)], h_send.at[n, k])
 
 
 def refit(limits, number, tokens, expert_ids, targets, gate_weight, up_weight, kept_units):
@@ -426,7 +433,7 @@
             pltpu.VMEM((ITERS, part, 2, 8, 128), f32),
             pltpu.VMEM((PLANE * part, 8, 128), f32),
             dma((4,)), dma, dma((5, 2)), dma, dma((5, 2)), dma((Z,)), dma((Z,)), dma((Z,)), dma((Z,)),
-            dma((Z,)), dma((Z,)), dma((3,)), dma((3,)), dma((3,)), dma((3,)),
+            dma((Z,)), dma((Z,)), dma((3,)), dma((3,)), dma((Z // 2, 3)), dma((Z // 2, 3)),
             dma((ITERS, part)), dma((ITERS, part)), dma, dma,
         ],
         compiler_params=pltpu.CompilerParams(

time: 150 us -> 134 us (0.89)
  Pallas kernels: 144 us -> 129 us
    pallas_call x1, Pallas kernels: 144 us -> 129 us  [refit(): pl.pallas_call(functools.partial(kernel, limits), out_shape=(jax.ShapeDty...]
where the time goes in v3:
time: 134 us
  Pallas kernels  129 us (96%)
  local copies, waits for them, and re-layouts  3.69 us (3%)
    pallas_call x1, Pallas kernels, refit(): pl.pallas_call(functools.partial(kernel, limits), out_shape=(jax.ShapeDty...  129 us

profile of v3, /device:TPU:1, one launch (start us, length us, event | category | flops | bytes accessed | tf_op | source)
XLA Modules:
  0.0 133.9 jit_solution(11151233644029698728)
XLA Ops:
  0.0 0.0 copy-start.4
  0.0 0.0 copy-start.1
  0.0 0.0 copy-start
  0.0 0.0 copy-start.3
  0.0 0.0 copy-start.2
  0.0 0.9 copy.11
  1.0 0.7 reshape.16.ids_ref
  1.6 129.2 %shard_map.66 = (f32[1,384,512]{2,1,0:T(8,128)S(1)}, f32[8,128]{1,0:T(8,128)}) custom-call(s32[1,512]{1,0:T(1,128)} %reshape.16.ids_ref, s32[1,384]{1,0:T(1,128)} %kept_ref.1, bf16[64,2048]{1,0:T(8,128)(2,1)} %tokens_hbm.1, bf16[512,2048]{1,0:T(8,128)(2,1)} %bitcast.7, bf16[512,768]{1,0:T(8,128)(2,1)} %bitcast.9, bf16[512,768]{1,0:T(8,128)(2,1)} %bitcast.5.up_hbm), custom_call_target="tpu_custom_call" | custom-call | tf_op jit(solution)/shard_map/pallas_call | solution.py:408
  130.8 1.2 slice.3
  132.7 0.0 copy-done.4
  132.7 0.0 copy-done.1
  132.7 0.0 copy-done
  132.7 0.0 copy-done.3
  132.7 0.0 copy-done.2
  132.7 0.3 conditional.1
  133.0 0.9 copy.16
Async XLA Ops:
  0.0 132.7 %copy-start.4 = (s32[1,384]{1,0:T(1,128)S(1)}, s32[1,384]{1,0:T(1,128)}, u32[]{:S(2)}) copy-start(s32[1,384]{1,0:T(1,128)} %kept_ref.1) | copy-start | bytes 4612
  0.0 132.7 %copy-start.1 = (bf16[1,512,768]{2,1,0:T(8,128)(2,1)S(1)}, bf16[1,512,768]{2,1,0:T(8,128)(2,1)}, u32[]{:S(2)}) copy-start(bf16[1,512,768]{2,1,0:T(8,128)(2,1)} %param.11) | copy-start | bytes 2359300
  0.0 132.7 %copy-start = (bf16[64,8,2048]{2,1,0:T(8,128)(2,1)S(1)}, bf16[64,8,2048]{2,1,0:T(8,128)(2,1)}, u32[]{:S(2)}) copy-start(bf16[64,8,2048]{2,1,0:T(8,128)(2,1)} %param.10) | copy-start | bytes 6291460
  0.0 132.7 %copy-start.3 = (s32[64,8]{0,1:T(8,128)S(1)}, s32[64,8]{0,1:T(8,128)}, u32[]{:S(2)}) copy-start(s32[64,8]{0,1:T(8,128)} %param.9) | copy-start | bytes 6148
  0.0 132.7 %copy-start.2 = (bf16[64,2048]{1,0:T(8,128)(2,1)S(1)}, bf16[64,2048]{1,0:T(8,128)(2,1)}, u32[]{:S(2)}) copy-start(bf16[64,2048]{1,0:T(8,128)(2,1)} %tokens_hbm.1) | copy-start | bytes 786436

commit v4 on v3

--- a/solution.py
+++ b/solution.py
@@ -22,7 +22,7 @@
 def kernel(
     limits, ids_ref, kept_ref, tokens_hbm, targets_hbm, gate_hbm, up_hbm, out_ref, flag_ref,
     tok, idsb, targ, gate, up, before, fsend, feats, weights, hid, tsend, tmid, tpack, tfin,
-    picked, rhs, system, vec_p, vec_s, scal, flags,
+    picked, rhs, system, vec_s, vec_q, vec_r, vec_w, vec_n, scal, flags,
     in_sem, ring_send, ring_recv, idr_send, idr_recv, f_send, f_recv, t1_send, t1_recv,
     t2_send, t2_recv, w_send, w_recv, h_send, h_recv, s_send, s_recv, g_send, g_recv,
 ):
@@ -50,20 +50,6 @@
     def drain(ref, sem):
         pltpu.make_async_copy(ref, ref, sem).wait()
 
-    barrier = pltpu.get_barrier_semaphore()
-
-    def greet_z(o, _):
-        pl.semaphore_signal(barrier, inc=1, device_id=at_z(o), device_id_type=MESH)
-        return 0
-
-    def greet_plane(k, _):
-        i2, d2 = in_plane(k)
-        pl.semaphore_signal(barrier, inc=1, device_id=(z * PLANE + i2, d2), device_id_type=MESH)
-        return 0
-
-    lax.fori_loop(1, Z, greet_z, 0)
-    lax.fori_loop(1, PLANE * L * C, greet_plane, 0)
-
     loads = [
         pltpu.make_async_copy(src, dst, in_sem.at[n])
         for n, (src, dst) in enumerate(
@@ -73,8 +59,30 @@
     for load in loads:
         load.start()
 
-    idsb[0] = jnp.broadcast_to(ids_ref[...], idsb.shape[1:])
+    barrier = pltpu.get_barrier_semaphore()
+
+    def greet_z(o, _):
+        pl.semaphore_signal(barrier, inc=1, device_id=at_z(o), device_id_type=MESH)
+        return 0
+
+    def greet_plane(k, _):
+        i2, d2 = in_plane(k)
+        pl.semaphore_signal(barrier, inc=1, device_id=(z * PLANE + i2, d2), device_id_type=MESH)
+        return 0
+
+    lax.fori_loop(1, Z, greet_z, 0)
+    lax.fori_loop(1, PLANE * L * C, greet_plane, 0)
+
     routes = idsb.shape[2]
+    per_token = ids_ref.shape[0]
+    place_at = lax.broadcasted_iota(jnp.int32, (tokens_here, routes), 1)
+    token_at = lax.broadcasted_iota(jnp.int32, (tokens_here, routes), 0)
+    wide = (place_at // per_token == token_at).astype(jnp.float32).astype(jnp.bfloat16)
+    every = dot(ids_ref[...].astype(jnp.float32).astype(jnp.bfloat16), wide)
+    place_at = lax.broadcasted_iota(jnp.int32, (per_token, routes), 1)
+    route_at = lax.broadcasted_iota(jnp.int32, (per_token, routes), 0)
+    ids_row = jnp.sum(jnp.where(place_at % per_token == route_at, every, 0.0), axis=0, keepdims=True)
+    idsb[0] = jnp.broadcast_to(ids_row, idsb.shape[1:]).astype(jnp.int32)
     row_at = lax.broadcasted_iota(jnp.int32, (routes, routes), 0)
     col_at = lax.broadcasted_iota(jnp.int32, (routes, routes), 1)
     before[...] = (row_at < col_at).astype(jnp.float32).astype(jnp.bfloat16)
@@ -291,6 +299,12 @@
     ring_wait_last()
     pack_features(7)
     pack_targets(7, Z // 2)
+    def tell(k, _):
+        i2, d2 = in_plane(k)
+        remote(flags.at[0], flags.at[k], g_send, g_recv, (z * PLANE + i2, d2)).start()
+        return 0
+
+    lax.fori_loop(1, PLANE * L * C, tell, 0)
     activate(2, 0)
     lax.fori_loop(0, 2, pass_on, 0)
     lax.fori_loop(3, 5, forward, 0)
@@ -308,12 +322,6 @@
     lax.fori_loop(0, 4, add_rhs, 0)
     forward(7, 0)
 
-    def tell(k, _):
-        i2, d2 = in_plane(k)
-        remote(flags.at[0], flags.at[k], g_send, g_recv, (z * PLANE + i2, d2)).start()
-        return 0
-
-    lax.fori_loop(1, PLANE * L * C, tell, 0)
     lax.fori_loop(2, 4, add_gram, 0)
     gram = system[...]
     on_diagonal = lax.broadcasted_iota(jnp.int32, gram.shape, 0) == lax.broadcasted_iota(jnp.int32, gram.shape, 1)
@@ -330,9 +338,12 @@
             total = total + rows[:, n * 128 : (n + 1) * 128]
         return total
 
-    def exchange(it, first, second):
-        scal[it, d, 0] = first
-        scal[it, d, 1] = second
+    def times_system(ref):
+        return jnp.dot(system[...], ref[...], precision=lax.Precision.HIGHEST)
+
+    def share(it, residual, image):
+        scal[it, d, 0] = folded(residual * residual)
+        scal[it, d, 1] = folded(residual * image)
         copies = []
         for k in range(1, L * C):
             there = (d + k) % (L * C)
@@ -341,6 +352,9 @@
             )
         for copy in copies:
             copy.start()
+        return copies
+
+    def collect(it, copies):
         for copy in copies:
             copy.wait()
         sums = scal[it, 0]
@@ -348,33 +362,32 @@
             sums = sums + scal[it, k]
         return jnp.sum(sums[0]), jnp.sum(sums[1])
 
-    rr_old = alpha = None
-    for it in range(ITERS):
-        residual = rhs[...]
-        image = jnp.dot(system[...], residual, precision=lax.Precision.HIGHEST)
-        rr, curve = exchange(it, folded(residual * residual), folded(residual * image))
-        if it == 0:
-            alpha = rr / curve
-            vec_p[...] = residual
-            vec_s[...] = image
-            out_ref[0] = alpha * residual
-            rhs[...] = residual - alpha * image
-        else:
-            beta = rr / rr_old
-            alpha = rr / (curve - beta * rr / alpha)
-            direction = residual + beta * vec_p[...]
-            out_ref[0] += alpha * direction
-            if it + 1 < ITERS:
-                applied = image + beta * vec_s[...]
-                vec_p[...] = direction
-                vec_s[...] = applied
-                rhs[...] = residual - alpha * applied
-        rr_old = rr
+    vec_s[...] = times_system(rhs)
+    copies = share(0, rhs[...], vec_s[...])
+    vec_q[...] = times_system(vec_s)
+    rr0, curve = collect(0, copies)
+    alpha0 = rr0 / curve
+    vec_r[...] = rhs[...] - alpha0 * vec_s[...]
+    vec_w[...] = vec_s[...] - alpha0 * vec_q[...]
+    copies = share(1, vec_r[...], vec_w[...])
+    vec_n[...] = times_system(vec_w)
+    rr1, curve = collect(1, copies)
+    beta1 = rr1 / rr0
+    alpha1 = rr1 / (curve - beta1 * rr1 / alpha0)
+    last = vec_r[...] - alpha1 * (vec_w[...] + beta1 * vec_s[...])
+    copies = share(2, last, vec_w[...] - alpha1 * (vec_n[...] + beta1 * vec_q[...]))
+    vec_n[...] = last
+    rr2, curve = collect(2, copies)
+    beta2 = rr2 / rr1
+    alpha2 = rr2 / (curve - beta2 * rr2 / alpha1)
+    of_r1 = alpha1 + alpha2 * beta2
+    of_r0 = alpha0 + of_r1 * beta1
+    out_ref[0] = of_r0 * rhs[...] + of_r1 * vec_r[...] + alpha2 * vec_n[...]
 
     others = flags.at[pl.ds(1, PLANE * L * C - 1)]
     drain(others, g_recv)
     drain(others, g_send)
-    flag_ref[...] = jnp.max(flags[...], axis=0)
+    flag_ref[0, 0] = (jnp.max(flags[...]) > 0).astype(jnp.int32)
 
     drain(tok.at[pl.ds(0, 7)], ring_send)
     drain(idsb.at[pl.ds(0, 7)], idr_send)
@@ -396,7 +409,7 @@
     routes = expert_ids.shape[1]
     keep = kept_units.shape[1]
     rows, units = gate_weight.shape[1:]
-    ids = expert_ids.reshape(1, -1)
+    ids = expert_ids.T
     targets = targets.reshape(-1, model_width)
     part = L * C
     out_cols = model_width // part
@@ -407,9 +420,9 @@
     bf, f32 = jnp.bfloat16, jnp.float32
     return pl.pallas_call(
         functools.partial(kernel, limits),
-        out_shape=(jax.ShapeDtypeStruct((1, keep, out_cols), f32), jax.ShapeDtypeStruct((8, 128), f32)),
+        out_shape=(jax.ShapeDtypeStruct((1, keep, out_cols), f32), jax.ShapeDtypeStruct((1, 1), jnp.int32)),
         in_specs=[vmem, vmem, hbm, hbm, hbm, hbm],
-        out_specs=(vmem, vmem),
+        out_specs=(vmem, pl.BlockSpec(memory_space=pltpu.SMEM)),
         scratch_shapes=[
             pltpu.VMEM((Z, tok_rows + spare, model_width), bf),
             pltpu.VMEM((Z, 8, tok_rows * routes), jnp.int32),
@@ -430,6 +443,9 @@
             pltpu.VMEM((keep, keep), f32),
             pltpu.VMEM((keep, out_cols), f32),
             pltpu.VMEM((keep, out_cols), f32),
+            pltpu.VMEM((keep, out_cols), f32),
+            pltpu.VMEM((keep, out_cols), f32),
+            pltpu.VMEM((keep, out_cols), f32),
             pltpu.VMEM((ITERS, part, 2, 8, 128), f32),
             pltpu.VMEM((PLANE * part, 8, 128), f32),
             dma((4,)), dma, dma((5, 2)), dma, dma((5, 2)), dma((Z,)), dma((Z,)), dma((Z,)), dma((Z,)),

time: 134 us -> 129 us (0.963)
  Pallas kernels: 129 us -> 126 us
  local copies, waits for them, and re-layouts: 3.69 us -> 0.91 us
    pallas_call x1, Pallas kernels: 129 us -> 126 us  [refit(): pl.pallas_call(functools.partial(kernel, limits), out_shape=(jax.ShapeDty...]
where the time goes in v4:
time: 129 us; the launch traced here: 128 us
  Pallas kernels  126 us (98%)
    pallas_call x1, Pallas kernels, refit(): pl.pallas_call(functools.partial(kernel, limits), out_shape=(jax.ShapeDty...  126 us

profile of v4, /device:TPU:1, one launch (start us, length us, event | category | flops | bytes accessed | tf_op | source)
XLA Modules:
  0.0 128.1 jit_solution(2226898433914873744)
XLA Ops:
  0.0 0.0 copy-start.5
  0.0 0.0 copy-start.2
  0.0 0.0 copy-start.1
  0.0 0.0 copy-start
  0.0 0.0 copy-start.4
  0.0 0.0 copy-start.3
  0.0 126.2 %shard_map.66 = (f32[1,384,512]{2,1,0:T(8,128)S(1)}, s32[1,1]{1,0:T(1,128)}) custom-call(s32[8,64]{1,0:T(8,128)} %bitcast.15, s32[1,384]{1,0:T(1,128)} %kept_ref.1, bf16[64,2048]{1,0:T(8,128)(2,1)} %tokens_hbm.1, bf16[512,2048]{1,0:T(8,128)(2,1)} %bitcast.9, bf16[512,768]{1,0:T(8,128)(2,1)} %bitcast.11, bf16[512,768]{1,0:T(8,128)(2,1)} %bitcast.13), custom_call_target="tpu_custom_call" | custom-call | tf_op jit(solution)/shard_map/pallas_call | solution.py:421
  126.8 0.0 copy-done.5
  126.8 0.0 copy-done.2
  126.9 0.0 copy-done.1
  126.9 0.0 copy-done
  126.9 0.0 copy-done.4
  126.9 0.0 copy-done.3
  126.9 0.3 conditional.1
  127.2 0.9 copy.12
Async XLA Ops:
  0.0 126.8 %copy-start.5 = (s32[1,384]{1,0:T(1,128)S(1)}, s32[1,384]{1,0:T(1,128)}, u32[]{:S(2)}) copy-start(s32[1,384]{1,0:T(1,128)} %kept_ref.1) | copy-start | bytes 4612
  0.0 126.8 %copy-start.2 = (bf16[1,512,768]{2,1,0:T(8,128)(2,1)S(1)}, bf16[1,512,768]{2,1,0:T(8,128)(2,1)}, u32[]{:S(2)}) copy-start(bf16[1,512,768]{2,1,0:T(8,128)(2,1)} %param.12) | copy-start | bytes 2359300
  0.0 126.9 %copy-start.1 = (bf16[1,512,768]{2,1,0:T(8,128)(2,1)S(1)}, bf16[1,512,768]{2,1,0:T(8,128)(2,1)}, u32[]{:S(2)}) copy-start(bf16[1,512,768]{2,1,0:T(8,128)(2,1)} %param.11) | copy-start | bytes 2359300
  0.0 126.9 %copy-start = (bf16[64,8,2048]{2,1,0:T(8,128)(2,1)S(1)}, bf16[64,8,2048]{2,1,0:T(8,128)(2,1)}, u32[]{:S(2)}) copy-start(bf16[64,8,2048]{2,1,0:T(8,128)(2,1)} %param.10) | copy-start | bytes 6291460
  0.0 126.9 %copy-start.4 = (s32[64,8]{0,1:T(8,128)S(1)}, s32[64,8]{0,1:T(8,128)}, u32[]{:S(2)}) copy-start(s32[64,8]{0,1:T(8,128)} %param.9) | copy-start | bytes 6148
  0.0 126.9 %copy-start.3 = (bf16[64,2048]{1,0:T(8,128)(2,1)S(1)}, bf16[64,2048]{1,0:T(8,128)(2,1)}, u32[]{:S(2)}) copy-start(bf16[64,2048]{1,0:T(8,128)(2,1)} %tokens_hbm.1) | copy-start | bytes 786436

commit v5 on v4

--- a/solution.py
+++ b/solution.py
@@ -24,7 +24,7 @@
     tok, idsb, targ, gate, up, before, fsend, feats, weights, hid, tsend, tmid, tpack, tfin,
     picked, rhs, system, vec_s, vec_q, vec_r, vec_w, vec_n, scal, flags,
     in_sem, ring_send, ring_recv, idr_send, idr_recv, f_send, f_recv, t1_send, t1_recv,
-    t2_send, t2_recv, w_send, w_recv, h_send, h_recv, s_send, s_recv, g_send, g_recv,
+    t2_send, t2_recv, w_send, w_recv, h_send, h_recv, s_send, s_recv, g_send, g_recv, v_send, v_recv,
 ):
     most, spare = limits
     tokens_here = tokens_hbm.shape[0]
@@ -83,6 +83,51 @@
     route_at = lax.broadcasted_iota(jnp.int32, (per_token, routes), 0)
     ids_row = jnp.sum(jnp.where(place_at % per_token == route_at, every, 0.0), axis=0, keepdims=True)
     idsb[0] = jnp.broadcast_to(ids_row, idsb.shape[1:]).astype(jnp.int32)
+
+    pl.semaphore_wait(barrier, Z - 1 + PLANE * L * C - 1)
+    loads[0].wait()
+
+    def pass_rows(first, count, step, send, recv):
+        if step < 4:
+            rows = pl.ds(first, count)
+            src_r, src_l = 2 * (step - 1), max(2 * step - 3, 0)
+            remote(tok.at[src_r, rows], tok.at[2 * step, rows], send, recv.at[step, 0], at_z(1)).start()
+            remote(tok.at[src_l, rows], tok.at[2 * step - 1, rows], send, recv.at[step, 1], at_z(Z - 1)).start()
+        else:
+            low, high = pl.ds(first, count // 2), pl.ds(first + count // 2, count // 2)
+            remote(tok.at[6, low], tok.at[7, low], send, recv.at[4, 0], at_z(1)).start()
+            remote(tok.at[5, high], tok.at[7, high], send, recv.at[4, 1], at_z(Z - 1)).start()
+
+    def take_rows(first, count, step, recv):
+        half = count // 2
+        of_r = tok.at[2 * step, pl.ds(first, count)] if step < 4 else tok.at[7, pl.ds(first, half)]
+        of_l = tok.at[2 * step - 1, pl.ds(first, count)] if step < 4 else tok.at[7, pl.ds(first + half, half)]
+        drain(of_r, recv.at[step, 0])
+        drain(of_l, recv.at[step, 1])
+
+    def ring_start(step):
+        pass_rows(0, tokens_here, step, ring_send, ring_recv)
+        src_r, src_l = 2 * (step - 1), max(2 * step - 3, 0)
+        to_r = 2 * step if step < 4 else 7
+        remote(idsb.at[src_r], idsb.at[to_r], idr_send, idr_recv.at[step, 0], at_z(1)).start()
+        if step < 4:
+            remote(idsb.at[src_l], idsb.at[2 * step - 1], idr_send, idr_recv.at[step, 1], at_z(Z - 1)).start()
+
+    def ring_wait(step):
+        take_rows(0, tokens_here, step, ring_recv)
+        drain(idsb.at[2 * step if step < 4 else 7], idr_recv.at[step, 0])
+        if step < 4:
+            drain(idsb.at[2 * step - 1], idr_recv.at[step, 1])
+
+    def spare_start(step):
+        if spare:
+            pass_rows(tokens_here, spare, step, v_send, v_recv)
+
+    def spare_wait(step):
+        if spare:
+            take_rows(tokens_here, spare, step, v_recv)
+
+    ring_start(1)
     row_at = lax.broadcasted_iota(jnp.int32, (routes, routes), 0)
     col_at = lax.broadcasted_iota(jnp.int32, (routes, routes), 1)
     before[...] = (row_at < col_at).astype(jnp.float32).astype(jnp.bfloat16)
@@ -116,36 +161,7 @@
     if spare:
         late_rows = pl.ds(tokens_here, spare)
         tok[0, late_rows] = dot(row_hot(my_row, float(most), spare), targ[...]).astype(jnp.bfloat16)
-
-    pl.semaphore_wait(barrier, Z - 1 + PLANE * L * C - 1)
-    loads[0].wait()
-
-    half = tok.shape[1] // 2
-
-    def ring_start(step):
-        src_r, src_l = 2 * (step - 1), jnp.maximum(2 * step - 3, 0)
-        remote(tok.at[src_r], tok.at[2 * step], ring_send, ring_recv.at[step, 0], at_z(1)).start()
-        remote(tok.at[src_l], tok.at[2 * step - 1], ring_send, ring_recv.at[step, 1], at_z(Z - 1)).start()
-        remote(idsb.at[src_r], idsb.at[2 * step], idr_send, idr_recv.at[step, 0], at_z(1)).start()
-        remote(idsb.at[src_l], idsb.at[2 * step - 1], idr_send, idr_recv.at[step, 1], at_z(Z - 1)).start()
-
-    def ring_wait(step):
-        drain(tok.at[2 * step], ring_recv.at[step, 0])
-        drain(tok.at[2 * step - 1], ring_recv.at[step, 1])
-        drain(idsb.at[2 * step], idr_recv.at[step, 0])
-        drain(idsb.at[2 * step - 1], idr_recv.at[step, 1])
-
-    low, high = pl.ds(0, half), pl.ds(half, half)
-
-    def ring_start_last():
-        remote(tok.at[6, low], tok.at[7, low], ring_send, ring_recv.at[4, 0], at_z(1)).start()
-        remote(tok.at[5, high], tok.at[7, high], ring_send, ring_recv.at[4, 1], at_z(Z - 1)).start()
-        remote(idsb.at[6], idsb.at[7], idr_send, idr_recv.at[4, 0], at_z(1)).start()
-
-    def ring_wait_last():
-        drain(tok.at[7, low], ring_recv.at[4, 0])
-        drain(tok.at[7, high], ring_recv.at[4, 1])
-        drain(idsb.at[7], idr_recv.at[4, 0])
+        spare_start(1)
 
     def pack_features(s):
         place = places(idsb[s], z * PLANE, PLANE)
@@ -209,7 +225,6 @@
     d_beside = l * C + (c + 1) % C
     d_diag = ((l + 1) % L) * C + (c + 1) % C
 
-    ring_start(1)
     spread(0, dot(pack_features(0), targ[...]))
 
     loads[2].wait()
@@ -276,12 +291,11 @@
 
     def turn(step):
         ring_wait(step)
-        if step < 3:
-            ring_start(step + 1)
-        else:
-            ring_start_last()
+        ring_start(step + 1)
         pack_features(2 * step - 1)
         pack_features(2 * step)
+        spare_wait(step)
+        spare_start(step + 1)
         pack_targets(2 * step - 1, step)
         hop_z(2 * step - 1, step, 2 * step)
         pack_targets(2 * step, Z - step)
@@ -296,7 +310,7 @@
     drain(weights.at[d_beside], w_recv.at[1])
     drain(weights.at[d_diag], w_recv.at[2])
     lax.fori_loop(0, 2, activate, 0)
-    ring_wait_last()
+    ring_wait(4)
     pack_features(7)
     pack_targets(7, Z // 2)
     def tell(k, _):
@@ -320,6 +334,7 @@
     rhs[...] = jnp.zeros_like(rhs)
     lax.fori_loop(0, 2, add_gram, 0)
     lax.fori_loop(0, 4, add_rhs, 0)
+    spare_wait(4)
     forward(7, 0)
 
     lax.fori_loop(2, 4, add_gram, 0)
@@ -356,7 +371,7 @@
 
     def collect(it, copies):
         for copy in copies:
-            copy.wait()
+            copy.wait_recv()
         sums = scal[it, 0]
         for k in range(1, L * C):
             sums = sums + scal[it, k]
@@ -389,7 +404,12 @@
     drain(others, g_send)
     flag_ref[0, 0] = (jnp.max(flags[...]) > 0).astype(jnp.int32)
 
-    drain(tok.at[pl.ds(0, 7)], ring_send)
+    for it in range(ITERS):
+        for k in range(1, L * C):
+            drain(scal.at[it, 0], s_send.at[it, k])
+    drain(tok.at[pl.ds(0, 7), pl.ds(0, tokens_here)], ring_send)
+    if spare:
+        drain(tok.at[pl.ds(0, 7), late_rows], v_send)
     drain(idsb.at[pl.ds(0, 7)], idr_send)
     for s in range(Z):
         drain(feats.at[s, pl.ds(0, (PLANE - 1) * CAP)], f_send.at[s])
@@ -450,7 +470,7 @@
             pltpu.VMEM((PLANE * part, 8, 128), f32),
             dma((4,)), dma, dma((5, 2)), dma, dma((5, 2)), dma((Z,)), dma((Z,)), dma((Z,)), dma((Z,)),
             dma((Z,)), dma((Z,)), dma((3,)), dma((3,)), dma((Z // 2, 3)), dma((Z // 2, 3)),
-            dma((ITERS, part)), dma((ITERS, part)), dma, dma,
+            dma((ITERS, part)), dma((ITERS, part)), dma, dma, dma, dma((5, 2)),
         ],
         compiler_params=pltpu.CompilerParams(
             collective_id=number, has_side_effects=True, vmem_limit_bytes=56 * 2**20

time: 129 us -> 127 us (0.984)
    pallas_call x1, Pallas kernels: 126 us -> 125 us  [refit(): pl.pallas_call(functools.partial(kernel, limits), out_shape=(jax.ShapeDty...]
where the time goes in v5:
time: 127 us
  Pallas kernels  125 us (98%)
    pallas_call x1, Pallas kernels, refit(): pl.pallas_call(functools.partial(kernel, limits), out_shape=(jax.ShapeDty...  125 us

profile of v5, /device:TPU:1, one launch (start us, length us, event | category | flops | bytes accessed | tf_op | source)
XLA Modules:
  0.0 126.5 jit_solution(15393727357969779663)
XLA Ops:
  0.0 0.0 copy-start.5
  0.0 0.0 copy-start.2
  0.0 0.0 copy-start.1
  0.0 0.0 copy-start
  0.0 0.0 copy-start.4
  0.0 0.0 copy-start.3
  0.0 124.7 %shard_map.66 = (f32[1,384,512]{2,1,0:T(8,128)S(1)}, s32[1,1]{1,0:T(1,128)}) custom-call(s32[8,64]{1,0:T(8,128)} %bitcast.15, s32[1,384]{1,0:T(1,128)} %kept_ref.1, bf16[64,2048]{1,0:T(8,128)(2,1)} %tokens_hbm.1, bf16[512,2048]{1,0:T(8,128)(2,1)} %bitcast.9, bf16[512,768]{1,0:T(8,128)(2,1)} %bitcast.11, bf16[512,768]{1,0:T(8,128)(2,1)} %bitcast.13), custom_call_target="tpu_custom_call" | custom-call | tf_op jit(solution)/shard_map/pallas_call | solution.py:441
  125.3 0.0 copy-done.5
  125.3 0.0 copy-done.2
  125.3 0.0 copy-done.1
  125.4 0.0 copy-done
  125.4 0.0 copy-done.4
  125.4 0.0 copy-done.3
  125.4 0.3 conditional.1
  125.7 0.9 copy.12
Async XLA Ops:
  0.0 125.3 %copy-start.5 = (s32[1,384]{1,0:T(1,128)S(1)}, s32[1,384]{1,0:T(1,128)}, u32[]{:S(2)}) copy-start(s32[1,384]{1,0:T(1,128)} %kept_ref.1) | copy-start | bytes 4612
  0.0 125.3 %copy-start.2 = (bf16[1,512,768]{2,1,0:T(8,128)(2,1)S(1)}, bf16[1,512,768]{2,1,0:T(8,128)(2,1)}, u32[]{:S(2)}) copy-start(bf16[1,512,768]{2,1,0:T(8,128)(2,1)} %param.12) | copy-start | bytes 2359300
  0.0 125.3 %copy-start.1 = (bf16[1,512,768]{2,1,0:T(8,128)(2,1)S(1)}, bf16[1,512,768]{2,1,0:T(8,128)(2,1)}, u32[]{:S(2)}) copy-start(bf16[1,512,768]{2,1,0:T(8,128)(2,1)} %param.11) | copy-start | bytes 2359300
  0.0 125.4 %copy-start = (bf16[64,8,2048]{2,1,0:T(8,128)(2,1)S(1)}, bf16[64,8,2048]{2,1,0:T(8,128)(2,1)}, u32[]{:S(2)}) copy-start(bf16[64,8,2048]{2,1,0:T(8,128)(2,1)} %param.10) | copy-start | bytes 6291460
  0.0 125.4 %copy-start.4 = (s32[64,8]{0,1:T(8,128)S(1)}, s32[64,8]{0,1:T(8,128)}, u32[]{:S(2)}) copy-start(s32[64,8]{0,1:T(8,128)} %param.9) | copy-start | bytes 6148
  0.0 125.4 %copy-start.3 = (bf16[64,2048]{1,0:T(8,128)(2,1)S(1)}, bf16[64,2048]{1,0:T(8,128)(2,1)}, u32[]{:S(2)}) copy-start(bf16[64,2048]{1,0:T(8,128)(2,1)} %tokens_hbm.1) | copy-start | bytes 786436
